TPU v7x, 32 devices: a whole 2x2x4 slice. The times are simulated.
32 devices in a mesh: dp: 8 (over z, core), proto: 4 (over y, x).
Axes of the slice: x: 2, y: 2, z: 4, core: 2. Of those that a mesh axis runs over, the one named last changes fastest.
Arguments:
- teacher_feat: bfloat16 [1024, 256], P('dp'), may hold values from -8 to 8
- student_feat: bfloat16 [5120, 256], P('dp'), may hold values from -8 to 8
- teacher_weight: bfloat16 [256, 131072], P(None, 'proto'), may hold values from -0.375 to 0.375
- head_weight: bfloat16 [256, 131072], P(None, 'proto'), may hold values from -0.375 to 0.375
- pairing: int32 [5120], P('dp'), may hold values from 0 to 1023, as said below
Outputs:
- student_grad: float32 [5120, 256], P('dp', 'proto')
- head_grad: float32 [256, 131072], P('dp', 'proto')
Inputs may be any that keep to these rules, and one draw needn't show every extreme that they name: `pairing`: row r among the 640 student rows of one index j of dp is crop r // 64 of image m = r mod 64; it names teacher row j * 128 + m + 64 * v with view v of 0 or 1; crop 0 takes view 1 and crop 1 takes view 0.
All inputs are finite; a program needn't handle non-finite values.
Results may differ from a plain program's by a relative error of at most 0.0022.
Values sent between devices are 32-bit elements; how exact they have to be, the bound alone decides.
A program may use at most 320 MiB of HBM per device.

v0:
```python
import functools
import math

import jax
import jax.numpy as jnp
from jax import lax
from jax.experimental import pallas as pl
from jax.experimental.pallas import tpu as pltpu
from jax.sharding import PartitionSpec as P

ITERS = 3


tiny_eps = 1e-06
teacher_temp = 0.04
student_temp = 0.1
BOTH = ("dp", "proto")


def unit_rows(values):
    floats = values.astype(jnp.float32)
    inverse = lax.rsqrt(jnp.sum(floats * floats, axis=1, keepdims=True) + tiny_eps)
    return (floats * inverse, inverse)


def unit_columns(values):
    floats = values.astype(jnp.float32)
    inverse = lax.rsqrt(jnp.sum(floats * floats, axis=0, keepdims=True) + tiny_eps)
    return (floats * inverse, inverse)


def dot(a, b, da, db):
    return lax.dot_general(a, b, (((da,), (db,)), ((), ())), preferred_element_type=jnp.float32)


def split_sum(values):
    high = values.astype(jnp.bfloat16)
    return high, (values - high.astype(jnp.float32)).astype(jnp.bfloat16)


LOG2E = math.log2(math.e)
MIB = 1 << 20


def diagonal():
    shape = (128, 128)
    return lax.broadcasted_iota(jnp.int32, shape, 0) == lax.broadcasted_iota(jnp.int32, shape, 1)


def to_lanes(column):
    return jnp.sum(jnp.where(diagonal(), column, 0.0), axis=0, keepdims=True)


def to_column(lanes):
    return jnp.sum(jnp.where(diagonal(), lanes, 0.0), axis=1, keepdims=True)


def chunks(size):
    step = min(size, 1024)
    return [(c, step) for c in range(0, size, step)]


def student_kernel(rows_ref, cols_ref, cols_t_ref, expo_ref, raw_ref, total_ref, kept_ref):
    rows = rows_ref[0].astype(jnp.bfloat16)
    kept_ref[...] = rows
    raw, total = None, None
    for start, step in chunks(cols_ref.shape[1]):
        logits = dot(rows, cols_ref[:, start : start + step], 1, 0)
        expo = jnp.exp2(logits * (LOG2E / student_temp))
        part = jnp.sum(expo, axis=1, keepdims=True)
        kept = expo.astype(jnp.bfloat16)
        expo_ref[:, start : start + step] = kept
        grad = dot(kept, cols_t_ref[start : start + step, :], 1, 0)
        total = part if total is None else total + part
        raw = grad if raw is None else raw + grad
    raw_ref[...] = raw.T
    for j in range(rows.shape[0] // 128):
        total_ref[0, j : j + 1, :] = to_lanes(total[j * 128 : (j + 1) * 128])


def student_pass(packet, stud, cols, cols_t):
    dp, _, width = packet.shape
    mine = cols.shape[1]
    return pl.pallas_call(
        student_kernel,
        grid=(dp,),
        in_specs=[
            pl.BlockSpec((1, stud, width), lambda i: (i, 0, 0)),
            pl.BlockSpec((width, mine), lambda i: (0, 0)),
            pl.BlockSpec((mine, width), lambda i: (0, 0)),
        ],
        out_specs=[
            pl.BlockSpec((stud, mine), lambda i: (i, 0)),
            pl.BlockSpec((width, stud), lambda i: (0, i)),
            pl.BlockSpec((1, stud // 128, 128), lambda i: (i, 0, 0)),
            pl.BlockSpec((stud, width), lambda i: (i, 0)),
        ],
        out_shape=[
            jax.ShapeDtypeStruct((dp * stud, mine), jnp.bfloat16),
            jax.ShapeDtypeStruct((width, dp * stud), jnp.float32),
            jax.ShapeDtypeStruct((dp, stud // 128, 128), jnp.float32),
            jax.ShapeDtypeStruct((dp * stud, width), jnp.bfloat16),
        ],
        compiler_params=pltpu.CompilerParams(vmem_limit_bytes=52 * MIB),
        cost_estimate=pl.CostEstimate(
            flops=4 * dp * stud * mine * width, bytes_accessed=2 * dp * stud * mine, transcendentals=dp * stud * mine
        ),
        name="student_pass",
    )(packet, cols, cols_t)


def positions():
    return {"dp": lax.axis_index("dp"), "proto": lax.axis_index("proto")}


def greet(here, sizes):
    barrier = pltpu.get_barrier_semaphore()
    for axis, size in sizes.items():
        for k in range(1, size):
            pl.semaphore_signal(
                barrier,
                inc=1,
                device_id={axis: lax.rem(here[axis] + k, size)},
                device_id_type=pl.DeviceIdType.MESH,
            )
    pl.semaphore_wait(barrier, sum(sizes.values()) - len(sizes))


def sends(here, sizes, axis, source, target, sems):
    copies = []
    for k in range(1, sizes[axis]):
        peer = lax.rem(here[axis] + k, sizes[axis])
        copies.append(
            pltpu.make_async_remote_copy(
                src_ref=source(peer),
                dst_ref=target(k),
                send_sem=sems.at[0, k],
                recv_sem=sems.at[1, k],
                device_id={axis: peer},
                device_id_type=pl.DeviceIdType.MESH,
            )
        )
    return copies


def start_all(copies):
    for copy in copies:
        copy.start()
    return copies


def wait_all(copies):
    for copy in copies:
        copy.wait()


def sinkhorn_kernel(
    dp,
    protos,
    rows_ref,
    cols_ref,
    part_ref,
    raw_ref,
    targets_ref,
    total_ref,
    raw_sum_ref,
    expo,
    cols,
    near,
    far,
    raw_in,
    near_sems,
    far_sems,
    raw_sems,
):
    here, sizes = positions(), {"dp": dp, "proto": protos}
    greet(here, sizes)
    share = raw_sum_ref.shape[0]

    def part_of(peer):
        return pl.ds(pl.multiple_of(peer * share, 8), share)

    raw_copies = start_all(
        sends(here, sizes, "proto", lambda peer: raw_ref.at[part_of(peer)], lambda k: raw_in.at[k], raw_sems)
    )
    count, mine = expo.shape
    blocks = count // 128

    def rows_at(block):
        return pl.ds(pl.multiple_of(block * 128, 128), 128)

    cols[...] = jnp.zeros_like(cols)

    @pl.loop(0, blocks)
    def _(block):
        at = rows_at(block)
        for start, step in chunks(mine):
            values = jnp.exp2(
                dot(rows_ref[at, :], cols_ref[:, start : start + step], 1, 0) * (LOG2E / teacher_temp)
            )
            expo[at, start : start + step] = values
            cols[:, start : start + step] += jnp.sum(values, axis=0, keepdims=True)

    def exchange(axis, buffer, sems, it, rows):
        wait_all(
            start_all(
                sends(
                    here,
                    sizes,
                    axis,
                    lambda peer: buffer.at[it, 0, pl.ds(0, rows)],
                    lambda k: buffer.at[it, k, pl.ds(0, rows)],
                    sems.at[it],
                )
            )
        )
        total = buffer[it, 0, 0:rows]
        for k in range(1, sizes[axis]):
            total = total + buffer[it, k, 0:rows]
        return total

    for it in range(ITERS):
        if it:
            cols[...] = jnp.zeros_like(cols)

            @pl.loop(0, blocks)
            def _(block):
                at = rows_at(block)
                scale = to_column(total_ref[pl.ds(block, 1), :])
                cols[...] += jnp.sum(expo[at, :] * scale, axis=0, keepdims=True)

        cols[...] = 1.0 / cols[...]

        @pl.loop(0, blocks)
        def _(block):
            sums = jnp.sum(expo[rows_at(block), :] * cols[...], axis=1, keepdims=True)
            near[it, 0, pl.ds(block, 1), :] = to_lanes(sums)

        used = blocks
        if it == 0:
            used = near.shape[2]
            near[0, 0, blocks:used, :] = part_ref[...]
        far[it, 0, 0:used] = exchange("proto", near, near_sems, it, used)
        total = exchange("dp", far, far_sems, it, used)
        total_ref[0:blocks, :] = 1.0 / total[0:blocks]
        if it == 0:
            total_ref[blocks:used, :] = total[blocks:used]

    @pl.loop(0, blocks)
    def _(block):
        at = rows_at(block)
        scale = to_column(total_ref[pl.ds(block, 1), :])
        targets_ref[at, :] = (expo[at, :] * scale * cols[...]).astype(jnp.bfloat16)

    wait_all(raw_copies)
    total = raw_ref[part_of(here["proto"]), :]
    for k in range(1, protos):
        total = total + raw_in[k]
    raw_sum_ref[...] = total


def sinkhorn(dp, protos, rows, cols, part, raw):
    count, mine = rows.shape[0], cols.shape[1]
    used = count // 128 + part.shape[0]
    vmem = pl.BlockSpec(memory_space=pltpu.VMEM)
    share = raw.shape[0] // protos
    targets, total, raw_sum = pl.pallas_call(
        functools.partial(sinkhorn_kernel, dp, protos),
        in_specs=[vmem] * 4,
        out_specs=[vmem] * 3,
        out_shape=[
            jax.ShapeDtypeStruct((count, mine), jnp.bfloat16),
            jax.ShapeDtypeStruct((used, 128), jnp.float32),
            jax.ShapeDtypeStruct((share, raw.shape[1]), jnp.float32),
        ],
        scratch_shapes=[
            pltpu.VMEM((count, mine), jnp.float32),
            pltpu.VMEM((1, mine), jnp.float32),
            pltpu.VMEM((ITERS, protos, used, 128), jnp.float32),
            pltpu.VMEM((ITERS, dp, used, 128), jnp.float32),
            pltpu.VMEM((protos, share, raw.shape[1]), jnp.float32),
            pltpu.SemaphoreType.DMA((ITERS, 2, protos)),
            pltpu.SemaphoreType.DMA((ITERS, 2, dp)),
            pltpu.SemaphoreType.DMA((2, protos)),
        ],
        compiler_params=pltpu.CompilerParams(
            collective_id=1, has_side_effects=True, vmem_limit_bytes=52 * MIB
        ),
        cost_estimate=pl.CostEstimate(
            flops=2 * count * mine * rows.shape[1], bytes_accessed=4 * count * mine, transcendentals=count * mine
        ),
        name="sinkhorn",
    )(rows, cols, part, raw)
    return targets, total[count // 128 :], raw_sum


def weight_kernel(
    dp,
    protos,
    steps,
    scale,
    expo_ref,
    targets_ref,
    head_ref,
    rows_ref,
    high_ref,
    low_ref,
    raw_ref,
    aim_ref,
    grad_ref,
    raw_own_ref,
    aim_own_ref,
    stage,
    raw_in,
    aim_near,
    aim_sum,
    aim_far,
    grad_sems,
    own_sem,
    raw_sems,
    near_sems,
    far_sems,
):
    here, sizes = positions(), {"dp": dp, "proto": protos}
    step = pl.program_id(0)
    share, stud = raw_own_ref.shape
    teach = aim_own_ref.shape[1]
    mine = stage.shape[1]
    size = head_ref.shape[1]
    depth = stage.shape[0] // dp

    def band(peer, height):
        return pl.ds(pl.multiple_of(peer * height, 8), height)

    def lanes(peer, length):
        return pl.ds(pl.multiple_of(peer * length, 128), length)

    raw_copies = sends(here, sizes, "dp", lambda e: raw_ref.at[:, lanes(e, stud)], lambda k: raw_in.at[k], raw_sems)
    near_copies = sends(here, sizes, "proto", lambda e: aim_ref.at[band(e, share)], lambda k: aim_near.at[k], near_sems)
    far_copies = sends(here, sizes, "dp", lambda e: aim_sum.at[:, lanes(e, teach)], lambda k: aim_far.at[k], far_sems)

    def columns(j):
        return pl.ds(pl.multiple_of(here["dp"] * mine + j * size, 128), size)

    def grad_copies(j):
        local = pl.ds(pl.multiple_of(j * size, 128), size)
        return sends(
            here,
            sizes,
            "dp",
            lambda e: stage.at[band(e, depth), local],
            lambda k: grad_ref.at[:, columns(j)],
            grad_sems.at[j],
        )

    @pl.when(step == 0)
    def _():
        greet(here, sizes)
        start_all(near_copies)
        start_all(raw_copies)

    targets = targets_ref[...]
    grad = dot(rows_ref[...], expo_ref[...], 1, 0) - dot(high_ref[...], targets, 1, 0) - dot(low_ref[...], targets, 1, 0)
    grad = grad * scale
    unit, inverse = unit_columns(head_ref[...])
    inner = jnp.sum(unit * grad, axis=0, keepdims=True)
    stage[:, pl.ds(pl.multiple_of(step * size, 128), size)] = (grad - unit * inner) * inverse
    start_all(grad_copies(step))

    @pl.when(step == steps - 1)
    def _():
        own = pltpu.make_async_copy(
            stage.at[band(here["dp"], depth)],
            grad_ref.at[:, pl.ds(pl.multiple_of(here["dp"] * mine, 128), mine)],
            own_sem,
        )
        own.start()
        wait_all(near_copies)
        total = aim_ref[band(here["proto"], share), :]
        for k in range(1, protos):
            total = total + aim_near[k]
        aim_sum[...] = total
        start_all(far_copies)
        wait_all(raw_copies)
        total = raw_ref[:, lanes(here["dp"], stud)]
        for k in range(1, dp):
            total = total + raw_in[k]
        raw_own_ref[...] = total
        wait_all(far_copies)
        total = aim_sum[:, lanes(here["dp"], teach)]
        for k in range(1, dp):
            total = total + aim_far[k]
        aim_own_ref[...] = total
        own.wait()
        for j in range(steps):
            wait_all(grad_copies(j))


def weight_pass(dp, protos, scale, expo, targets, head, rows, high, low, raw, aim):
    width, mine = head.shape
    count, teach = rows.shape[1], high.shape[1]
    size = min(mine, 512)
    steps = mine // size
    share = raw.shape[0]

    def whole(array):
        return pl.BlockSpec(array.shape, lambda i: (0, 0))

    def block(array):
        return pl.BlockSpec((array.shape[0], size), lambda i: (0, i))

    own = [(share, count // dp), (share, teach // dp)]
    return pl.pallas_call(
        functools.partial(weight_kernel, dp, protos, steps, scale),
        grid=(steps,),
        in_specs=[block(expo), block(targets), block(head)] + [whole(x) for x in (rows, high, low, raw, aim)],
        out_specs=[pl.BlockSpec(memory_space=pl.ANY)] + [pl.BlockSpec(shape, lambda i: (0, 0)) for shape in own],
        out_shape=[jax.ShapeDtypeStruct(shape, jnp.float32) for shape in [(width // dp, dp * mine)] + own],
        scratch_shapes=[
            pltpu.VMEM((width, mine), jnp.float32),
            pltpu.VMEM((dp,) + own[0], jnp.float32),
            pltpu.VMEM((protos, share, teach), jnp.float32),
            pltpu.VMEM((share, teach), jnp.float32),
            pltpu.VMEM((dp,) + own[1], jnp.float32),
            pltpu.SemaphoreType.DMA((steps, 2, dp)),
            pltpu.SemaphoreType.DMA,
            pltpu.SemaphoreType.DMA((2, dp)),
            pltpu.SemaphoreType.DMA((2, protos)),
            pltpu.SemaphoreType.DMA((2, dp)),
        ],
        compiler_params=pltpu.CompilerParams(
            collective_id=2, has_side_effects=True, vmem_limit_bytes=52 * MIB
        ),
        cost_estimate=pl.CostEstimate(
            flops=2 * count * mine * width, bytes_accessed=2 * count * mine, transcendentals=0
        ),
        name="weight_pass",
    )(expo, targets, head, rows, high, low, raw, aim)


def body(teacher_feat, student_feat, teacher_weight, head_weight, pairing):
    dp, me = lax.axis_size("dp"), lax.axis_index("dp")
    protos = lax.axis_size("proto")
    teach, width = teacher_feat.shape
    stud = student_feat.shape[0]
    images = teach // 2
    crops = stud // images
    mine = head_weight.shape[1] // dp
    scale = 1.0 / (student_temp * stud * dp)

    teach_unit = unit_rows(teacher_feat)[0]
    stud_unit, stud_inverse = unit_rows(student_feat)
    view = (pairing - me * teach) // images
    kept = stud_unit.astype(jnp.bfloat16).astype(jnp.float32).reshape(crops, images, width)
    second = (view == 1).reshape(crops, images, 1)
    pair_sums = jnp.concatenate(
        [jnp.sum(jnp.where(second, 0.0, kept), 0), jnp.sum(jnp.where(second, kept, 0.0), 0)], 0
    )
    packet = jnp.concatenate([stud_unit, teach_unit, pair_sums], 0)
    packet = lax.optimization_barrier(lax.all_gather(packet, "dp", axis=0, tiled=False))
    teach_rows = packet[:, stud : stud + teach].reshape(dp * teach, width).astype(jnp.bfloat16)
    sums = packet[:, stud + teach :].reshape(dp * teach, width)

    teach_cols = unit_columns(lax.dynamic_slice_in_dim(teacher_weight, me * mine, mine, 1))[0].astype(jnp.bfloat16)
    own_head = lax.dynamic_slice_in_dim(head_weight, me * mine, mine, 1)
    head_cols = unit_columns(own_head)[0].astype(jnp.bfloat16)

    expo_s, raw, part, stud_rows = student_pass(packet, stud, head_cols, head_cols.T)
    targets, totals, raw = sinkhorn(
        dp, protos, teach_rows, teach_cols, part.reshape(dp * stud // 128, 128), raw
    )
    totals = totals.reshape(dp, stud)
    aim = dot(head_cols, targets, 1, 1)
    scaled = (stud_rows.astype(jnp.float32) / totals.reshape(dp * stud, 1)).astype(jnp.bfloat16)
    high, low = split_sum(sums.T)
    head_grad, raw, aim = weight_pass(
        dp, protos, scale, expo_s, targets, own_head, scaled.T, high, low, raw, aim
    )

    share = width // protos
    offset = lax.axis_index("proto") * share
    view_lanes = (view == 1).reshape(1, crops, images)
    aims = aim.reshape(share, 2, 1, images)
    picked = jnp.where(view_lanes, aims[:, 1], aims[:, 0]).reshape(share, stud)
    own_part = (raw / lax.dynamic_index_in_dim(totals, me, 0, True) - picked) * scale
    own_unit = lax.dynamic_slice_in_dim(stud_unit, offset, share, 1).T
    along = lax.psum(jnp.sum(own_unit * own_part, axis=0, keepdims=True), "proto")
    student_grad = (own_part - own_unit * along).T * stud_inverse
    return (student_grad, head_grad)


def solution(mesh):
    return jax.shard_map(
        body,
        mesh=mesh,
        in_specs=(P("dp", None), P("dp", None), P(None, "proto"), P(None, "proto"), P("dp")),
        out_specs=(P("dp", "proto"), P("dp", "proto")),
        check_vma=False,
    )
```

profile of v0, /device:TPU:8, one launch (start us, length us, event | category | flops | bytes accessed | tf_op | source)
XLA Modules:
  0.0 408.3 jit_solution(7442722348938513959)
XLA Ops:
  7.2 0.0 all-gather.3.cloned.1.call-start
  7.2 0.7 fusion.15
  7.9 0.1 broadcast_in_dim.61
  8.0 0.9 copy.25
  9.0 0.1 fusion.13
  9.0 1.2 copy.24
  10.2 0.1 fusion.8
  10.3 0.1 convert_convert_fusion
  10.4 0.2 copy.26
  10.7 0.2 select_reduce_fusion.1
  10.8 0.1 copy.27
  10.9 0.1 copy.28
  11.0 1.0 pad_maximum_fusion
  12.1 0.0 all-gather.3.cloned.1.call-update
  12.1 3.2 fusion
  15.3 0.0 copy-start.2
  15.3 2.0 fusion.22
  17.3 4.1 copy.30.cols_t_ref
  21.3 3.6 fusion.3.cols_ref
  24.9 0.0 copy-done.2
  24.9 1.8 fusion.1.cols_ref
  26.7 57.5 %all-gather.3.cloned.1.call-done = f32[7168,256]{0,1:T(8,128)} async-done(((f32[896,256]{0,1:T(8,128)}), f32[7168,256]{0,1:T(8,128)}) %all-gather.3.cloned.1.call-update) | async-done | bytes 7340048 | tf_op jit(solution)/shard_map/all_gather | solution.py:460
  84.2 4.4 %copy.37 = f32[32,8,8,896]{3,2,1,0:T(8,128)S(1)} copy(f32[32,8,8,896]{3,1,2,0:T(8,128)} %bitcast.63) | data formatting | bytes 14680064
  88.6 0.0 copy-start.1
  88.6 0.1 slice.27
  88.7 2.9 copy-done.1
  91.6 0.1 slice.22
  91.6 8.6 %copy.29.rows_ref = f32[8,896,256]{2,1,0:T(8,128)} copy(f32[8,896,256]{1,0,2:T(8,128)} %bitcast.60) | data formatting | bytes 14680064 | tf_op jit(solution)/shard_map/optimization_barrier | solution.py:460
  100.2 0.2 fusion.7.low_ref
  100.4 0.2 copy.43
  100.6 0.3 copy.31
  101.0 34.6 %student_pass.1 = (bf16[5120,4096]{1,0:T(8,128)(2,1)}, f32[256,5120]{1,0:T(8,128)}, f32[8,5,128]{2,1,0:T(8,128)S(1)}, bf16[5120,256]{1,0:T(8,128)(2,1)}) custom-call(f32[8,896,256]{2,1,0:T(8,128)} %copy.29.rows_ref, bf16[256,4096]{1,0:T(8,128)(2,1)} %fusion.1.cols_ref, bf16[4096,256]{1,0:T(8,128)(2,1)} %copy.30.cols_t_ref), custom_call_target="tpu_custom_call" | custom-call | flops 21474836480 | bytes 41943040 | tf_op jit(solution)/shard_map/student_pass/pallas_call | solution.py:84
  135.6 0.0 copy-start.3
  135.6 101.6 %sinkhorn.1 = (bf16[1024,4096]{1,0:T(8,128)(2,1)}, f32[48,128]{1,0:T(8,128)S(1)}, f32[64,5120]{1,0:T(8,128)S(1)}) custom-call(bf16[1024,256]{1,0:T(8,128)(2,1)S(1)} %bitcast.57, bf16[256,4096]{1,0:T(8,128)(2,1)} %fusion.3.cols_ref, f32[40,128]{1,0:T(8,128)S(1)} %reshape.62.part_ref, f32[256,5120]{1,0:T(8,128)} %get-tuple-element.14.raw_ref), custom_call_target="tpu_custom_call" | custom-call | flops 2147483648 | bytes 16777216 | tf_op jit(solution)/shard_map/sinkhorn/pallas_call | solution.py:267
  237.2 0.0 copy-start
  237.2 0.0 copy-done.3
  237.2 7.2 %fusion.19.aim_ref = f32[256,1024]{1,0:T(8,128)} fusion(bf16[256,4096]{1,0:T(8,128)(2,1)S(1)} %copy-done.3, bf16[1024,4096]{1,0:T(8,128)(2,1)} %get-tuple-element.15.targets_ref), kind=kOutput, calls=%fused_computation.49 | convolution fusion | flops 2147483648 | bytes 11534336 | tf_op jit(solution)/shard_map/dot_general | solution.py:33
  244.4 0.0 copy-done
  244.4 4.5 %copy.32 = bf16[5120,256]{0,1:T(8,128)(2,1)} copy(bf16[5120,256]{1,0:T(8,128)(2,1)} %get-tuple-element.16) | data formatting | bytes 5242880 | tf_op jit(solution)/shard_map/student_pass/pallas_call | solution.py:84
  248.9 3.8 fusion.4.rows_ref
  252.7 133.5 %weight_pass.1 = (f32[32,32768]{1,0:T(8,128)}, f32[64,640]{1,0:T(8,128)S(1)}, f32[64,128]{1,0:T(8,128)S(1)}) custom-call(bf16[5120,4096]{1,0:T(8,128)(2,1)} %get-tuple-element.12.expo_ref, bf16[1024,4096]{1,0:T(8,128)(2,1)} %get-tuple-element.15.targets_ref, bf16[256,4096]{1,0:T(8,128)(2,1)} %copy-done.2, bf16[256,5120]{1,0:T(8,128)(2,1)} %fusion.4.rows_ref, ...), custom_call_target="tpu_custom_call" | custom-call | flops 10737418240 | bytes 41943040 | tf_op jit(solution)/shard_map/weight_pass/pallas_call | solution.py:413
  386.3 0.1 reshape.65
  386.4 0.1 fusion.17
  386.4 0.1 copy.34
  386.5 0.1 copy.33
  386.6 0.1 copy.35
  386.8 0.1 copy.36
  387.0 0.1 fusion.9
  387.1 9.3 %psum.7 = f32[640]{0:T(1024)S(1)} all-reduce(f32[640]{0:T(1024)S(1)} %get-tuple-element.24), channel_id=1, replica_groups=mesh['dp'=8,'proto'=4] {'proto'}, use_global_device_ids=true, to_apply=%region_7.8 | all-reduce | flops 640 | bytes 5120 | tf_op jit(solution)/shard_map/psum | solution.py:487
  396.3 0.7 fusion.12
  397.0 4.5 %copy.45 = f32[32,32768]{1,0:T(8,128)} copy(f32[32,32768]{1,0:T(8,128)} %get-tuple-element.38) | data formatting | bytes 8388608
  (11 shorter events, 0.2 us)
Async XLA Ops:
  7.2 77.0 %all-gather.3.cloned.1.call-start = ((), (), s32[]{:S(2)}) async-start(), calls=%async_computation | async-start | bytes 8257536 | tf_op jit(solution)/shard_map/all_gather | solution.py:460
  15.3 9.7 %copy-start.2 = (bf16[256,4096]{1,0:T(8,128)(2,1)}, bf16[256,4096]{1,0:T(8,128)(2,1)S(1)}, u32[]{:S(2)}) copy-start(bf16[256,4096]{1,0:T(8,128)(2,1)S(1)} %get-tuple-element.27.head_ref) | copy-start | bytes 6291460
  88.6 3.0 copy-start.1
  135.6 101.6 %copy-start.3 = (bf16[256,4096]{1,0:T(8,128)(2,1)S(1)}, bf16[256,4096]{1,0:T(8,128)(2,1)}, u32[]{:S(2)}) copy-start(bf16[256,4096]{1,0:T(8,128)(2,1)} %fusion.1.cols_ref) | copy-start | bytes 6291460
  237.2 7.2 %copy-start = (f32[64,5120]{1,0:T(8,128)}, f32[64,5120]{1,0:T(8,128)S(1)}, u32[]{:S(2)}) copy-start(f32[64,5120]{1,0:T(8,128)S(1)} %get-tuple-element.18.raw_ref) | copy-start | bytes 3932164
Sparse Core Ops, SparseCore 0:
  12.2 71.9 all-gather.2
where the time goes:
time: 410 us; the launch traced here: 408 us
  Pallas kernels  270 us (66%)
  waiting for transfers between devices  57.5 us (14%)
  local copies, waits for them, and re-layouts  32.9 us (8%)
  other arithmetic  17.5 us (4%)
  between operations  14.2 us (3%)
  blocking collectives  9.25 us (2%)
  matrix products  7.18 us (2%)
    pallas_call x1, Pallas kernels, weight_pass(): pl.pallas_call(functools.partial(weight_kernel, dp, protos, steps, scale)...  134 us
    pallas_call x1, Pallas kernels, sinkhorn(): pl.pallas_call(functools.partial(sinkhorn_kernel, dp, protos), in_specs=[...  102 us
    all_gather x1, waiting for transfers between devices, body(): lax.all_gather(packet, 'dp', axis=0, tiled=False)  57.5 us
    pallas_call x1, Pallas kernels, student_pass(): pl.pallas_call(student_kernel, grid=(dp,), in_specs=[pl.BlockSpec((1, stu...  34.6 us
    unnamed x13, local copies, waits for them, and re-layouts  14.1 us
    psum x1, blocking collectives, body(): lax.psum(jnp.sum(own_unit * own_part, axis=0, keepdims=True), 'proto')  9.25 us
    optimization_barrier x1, local copies, waits for them, and re-layouts, body(): lax.optimization_barrier(lax.all_gather(packet, 'dp', axis=0, tiled=False))  8.58 us
  transfers between devices with their start and end apart: 1, of which 1 were waited for; matrix products, arithmetic and copies ran while one was open for 4% of the time, Pallas kernels for 0%

commit v1 on v0

--- a/solution.py
+++ b/solution.py
@@ -60,9 +60,24 @@
     return [(c, step) for c in range(0, size, step)]
 
 
-def student_kernel(rows_ref, cols_ref, cols_t_ref, expo_ref, raw_ref, total_ref, kept_ref):
+def student_kernel(
+    rows_ref,
+    teach_ref,
+    sums_ref,
+    cols_ref,
+    cols_t_ref,
+    expo_ref,
+    raw_ref,
+    total_ref,
+    kept_ref,
+    teach_rows_ref,
+    high_ref,
+    low_ref,
+):
     rows = rows_ref[0].astype(jnp.bfloat16)
-    kept_ref[...] = rows
+    kept_ref[...] = rows_ref[0].T.astype(jnp.bfloat16)
+    teach_rows_ref[...] = teach_ref[0].astype(jnp.bfloat16)
+    high_ref[...], low_ref[...] = split_sum(sums_ref[0].T)
     raw, total = None, None
     for start, step in chunks(cols_ref.shape[1]):
         logits = dot(rows, cols_ref[:, start : start + step], 1, 0)
@@ -78,14 +93,18 @@
         total_ref[0, j : j + 1, :] = to_lanes(total[j * 128 : (j + 1) * 128])
 
 
-def student_pass(packet, stud, cols, cols_t):
+def student_pass(packet, stud, teach, cols, cols_t):
     dp, _, width = packet.shape
+    first = stud // teach
+    assert stud == first * teach
     mine = cols.shape[1]
     return pl.pallas_call(
         student_kernel,
         grid=(dp,),
         in_specs=[
             pl.BlockSpec((1, stud, width), lambda i: (i, 0, 0)),
+            pl.BlockSpec((1, teach, width), lambda i: (i, first, 0)),
+            pl.BlockSpec((1, teach, width), lambda i: (i, first + 1, 0)),
             pl.BlockSpec((width, mine), lambda i: (0, 0)),
             pl.BlockSpec((mine, width), lambda i: (0, 0)),
         ],
@@ -93,20 +112,26 @@
             pl.BlockSpec((stud, mine), lambda i: (i, 0)),
             pl.BlockSpec((width, stud), lambda i: (0, i)),
             pl.BlockSpec((1, stud // 128, 128), lambda i: (i, 0, 0)),
-            pl.BlockSpec((stud, width), lambda i: (i, 0)),
+            pl.BlockSpec((width, stud), lambda i: (0, i)),
+            pl.BlockSpec((teach, width), lambda i: (i, 0)),
+            pl.BlockSpec((width, teach), lambda i: (0, i)),
+            pl.BlockSpec((width, teach), lambda i: (0, i)),
         ],
         out_shape=[
             jax.ShapeDtypeStruct((dp * stud, mine), jnp.bfloat16),
             jax.ShapeDtypeStruct((width, dp * stud), jnp.float32),
             jax.ShapeDtypeStruct((dp, stud // 128, 128), jnp.float32),
-            jax.ShapeDtypeStruct((dp * stud, width), jnp.bfloat16),
+            jax.ShapeDtypeStruct((width, dp * stud), jnp.bfloat16),
+            jax.ShapeDtypeStruct((dp * teach, width), jnp.bfloat16),
+            jax.ShapeDtypeStruct((width, dp * teach), jnp.bfloat16),
+            jax.ShapeDtypeStruct((width, dp * teach), jnp.bfloat16),
         ],
         compiler_params=pltpu.CompilerParams(vmem_limit_bytes=52 * MIB),
         cost_estimate=pl.CostEstimate(
             flops=4 * dp * stud * mine * width, bytes_accessed=2 * dp * stud * mine, transcendentals=dp * stud * mine
         ),
         name="student_pass",
-    )(packet, cols, cols_t)
+    )(packet, packet, packet, cols, cols_t)
 
 
 def positions():
@@ -160,29 +185,17 @@
     rows_ref,
     cols_ref,
     part_ref,
-    raw_ref,
     targets_ref,
     total_ref,
-    raw_sum_ref,
     expo,
     cols,
     near,
     far,
-    raw_in,
     near_sems,
     far_sems,
-    raw_sems,
 ):
     here, sizes = positions(), {"dp": dp, "proto": protos}
     greet(here, sizes)
-    share = raw_sum_ref.shape[0]
-
-    def part_of(peer):
-        return pl.ds(pl.multiple_of(peer * share, 8), share)
-
-    raw_copies = start_all(
-        sends(here, sizes, "proto", lambda peer: raw_ref.at[part_of(peer)], lambda k: raw_in.at[k], raw_sems)
-    )
     count, mine = expo.shape
     blocks = count // 128
 
@@ -252,36 +265,26 @@
         scale = to_column(total_ref[pl.ds(block, 1), :])
         targets_ref[at, :] = (expo[at, :] * scale * cols[...]).astype(jnp.bfloat16)
 
-    wait_all(raw_copies)
-    total = raw_ref[part_of(here["proto"]), :]
-    for k in range(1, protos):
-        total = total + raw_in[k]
-    raw_sum_ref[...] = total
-
-
-def sinkhorn(dp, protos, rows, cols, part, raw):
+
+def sinkhorn(dp, protos, rows, cols, part):
     count, mine = rows.shape[0], cols.shape[1]
     used = count // 128 + part.shape[0]
     vmem = pl.BlockSpec(memory_space=pltpu.VMEM)
-    share = raw.shape[0] // protos
-    targets, total, raw_sum = pl.pallas_call(
+    targets, total = pl.pallas_call(
         functools.partial(sinkhorn_kernel, dp, protos),
-        in_specs=[vmem] * 4,
-        out_specs=[vmem] * 3,
+        in_specs=[vmem] * 3,
+        out_specs=[vmem] * 2,
         out_shape=[
             jax.ShapeDtypeStruct((count, mine), jnp.bfloat16),
             jax.ShapeDtypeStruct((used, 128), jnp.float32),
-            jax.ShapeDtypeStruct((share, raw.shape[1]), jnp.float32),
         ],
         scratch_shapes=[
             pltpu.VMEM((count, mine), jnp.float32),
             pltpu.VMEM((1, mine), jnp.float32),
             pltpu.VMEM((ITERS, protos, used, 128), jnp.float32),
             pltpu.VMEM((ITERS, dp, used, 128), jnp.float32),
-            pltpu.VMEM((protos, share, raw.shape[1]), jnp.float32),
             pltpu.SemaphoreType.DMA((ITERS, 2, protos)),
             pltpu.SemaphoreType.DMA((ITERS, 2, dp)),
-            pltpu.SemaphoreType.DMA((2, protos)),
         ],
         compiler_params=pltpu.CompilerParams(
             collective_id=1, has_side_effects=True, vmem_limit_bytes=52 * MIB
@@ -290,8 +293,8 @@
             flops=2 * count * mine * rows.shape[1], bytes_accessed=4 * count * mine, transcendentals=count * mine
         ),
         name="sinkhorn",
-    )(rows, cols, part, raw)
-    return targets, total[count // 128 :], raw_sum
+    )(rows, cols, part)
+    return targets, total[count // 128 :]
 
 
 def weight_kernel(
@@ -311,13 +314,16 @@
     raw_own_ref,
     aim_own_ref,
     stage,
-    raw_in,
+    raw_near,
+    raw_sum,
+    raw_far,
     aim_near,
     aim_sum,
     aim_far,
     grad_sems,
     own_sem,
-    raw_sems,
+    raw_near_sems,
+    raw_far_sems,
     near_sems,
     far_sems,
 ):
@@ -335,7 +341,22 @@
     def lanes(peer, length):
         return pl.ds(pl.multiple_of(peer * length, 128), length)
 
-    raw_copies = sends(here, sizes, "dp", lambda e: raw_ref.at[:, lanes(e, stud)], lambda k: raw_in.at[k], raw_sems)
+    raw_copies = sends(
+        here, sizes, "dp", lambda e: raw_sum.at[:, lanes(e, stud)], lambda k: raw_far.at[k], raw_far_sems
+    )
+    each = dp // steps
+
+    def block_copies(j):
+        at = pl.ds(pl.multiple_of(j * each * stud, 128), each * stud)
+        return sends(
+            here,
+            sizes,
+            "proto",
+            lambda e: raw_ref.at[band(e, share), at],
+            lambda k: raw_near.at[k, :, at],
+            raw_near_sems.at[j],
+        )
+
     near_copies = sends(here, sizes, "proto", lambda e: aim_ref.at[band(e, share)], lambda k: aim_near.at[k], near_sems)
     far_copies = sends(here, sizes, "dp", lambda e: aim_sum.at[:, lanes(e, teach)], lambda k: aim_far.at[k], far_sems)
 
@@ -357,7 +378,6 @@
     def _():
         greet(here, sizes)
         start_all(near_copies)
-        start_all(raw_copies)
 
     targets = targets_ref[...]
     grad = dot(rows_ref[...], expo_ref[...], 1, 0) - dot(high_ref[...], targets, 1, 0) - dot(low_ref[...], targets, 1, 0)
@@ -366,6 +386,7 @@
     inner = jnp.sum(unit * grad, axis=0, keepdims=True)
     stage[:, pl.ds(pl.multiple_of(step * size, 128), size)] = (grad - unit * inner) * inverse
     start_all(grad_copies(step))
+    start_all(block_copies(step))
 
     @pl.when(step == steps - 1)
     def _():
@@ -381,10 +402,17 @@
             total = total + aim_near[k]
         aim_sum[...] = total
         start_all(far_copies)
+        for j in range(steps):
+            wait_all(block_copies(j))
+        total = raw_ref[band(here["proto"], share), :]
+        for k in range(1, protos):
+            total = total + raw_near[k]
+        raw_sum[...] = total
+        start_all(raw_copies)
         wait_all(raw_copies)
-        total = raw_ref[:, lanes(here["dp"], stud)]
+        total = raw_sum[:, lanes(here["dp"], stud)]
         for k in range(1, dp):
-            total = total + raw_in[k]
+            total = total + raw_far[k]
         raw_own_ref[...] = total
         wait_all(far_copies)
         total = aim_sum[:, lanes(here["dp"], teach)]
@@ -401,7 +429,8 @@
     count, teach = rows.shape[1], high.shape[1]
     size = min(mine, 512)
     steps = mine // size
-    share = raw.shape[0]
+    assert dp % steps == 0
+    share = width // protos
 
     def whole(array):
         return pl.BlockSpec(array.shape, lambda i: (0, 0))
@@ -413,17 +442,22 @@
     return pl.pallas_call(
         functools.partial(weight_kernel, dp, protos, steps, scale),
         grid=(steps,),
-        in_specs=[block(expo), block(targets), block(head)] + [whole(x) for x in (rows, high, low, raw, aim)],
+        in_specs=[block(expo), block(targets), block(head)]
+        + [whole(x) for x in (rows, high, low)]
+        + [pl.BlockSpec(memory_space=pltpu.VMEM)] * 2,
         out_specs=[pl.BlockSpec(memory_space=pl.ANY)] + [pl.BlockSpec(shape, lambda i: (0, 0)) for shape in own],
         out_shape=[jax.ShapeDtypeStruct(shape, jnp.float32) for shape in [(width // dp, dp * mine)] + own],
         scratch_shapes=[
             pltpu.VMEM((width, mine), jnp.float32),
+            pltpu.VMEM((protos, share, count), jnp.float32),
+            pltpu.VMEM((share, count), jnp.float32),
             pltpu.VMEM((dp,) + own[0], jnp.float32),
             pltpu.VMEM((protos, share, teach), jnp.float32),
             pltpu.VMEM((share, teach), jnp.float32),
             pltpu.VMEM((dp,) + own[1], jnp.float32),
             pltpu.SemaphoreType.DMA((steps, 2, dp)),
             pltpu.SemaphoreType.DMA,
+            pltpu.SemaphoreType.DMA((steps, 2, protos)),
             pltpu.SemaphoreType.DMA((2, dp)),
             pltpu.SemaphoreType.DMA((2, protos)),
             pltpu.SemaphoreType.DMA((2, dp)),
@@ -457,24 +491,20 @@
         [jnp.sum(jnp.where(second, 0.0, kept), 0), jnp.sum(jnp.where(second, kept, 0.0), 0)], 0
     )
     packet = jnp.concatenate([stud_unit, teach_unit, pair_sums], 0)
-    packet = lax.optimization_barrier(lax.all_gather(packet, "dp", axis=0, tiled=False))
-    teach_rows = packet[:, stud : stud + teach].reshape(dp * teach, width).astype(jnp.bfloat16)
-    sums = packet[:, stud + teach :].reshape(dp * teach, width)
-
+    packet = lax.all_gather(packet, "dp", axis=0, tiled=False)
     teach_cols = unit_columns(lax.dynamic_slice_in_dim(teacher_weight, me * mine, mine, 1))[0].astype(jnp.bfloat16)
     own_head = lax.dynamic_slice_in_dim(head_weight, me * mine, mine, 1)
     head_cols = unit_columns(own_head)[0].astype(jnp.bfloat16)
 
-    expo_s, raw, part, stud_rows = student_pass(packet, stud, head_cols, head_cols.T)
-    targets, totals, raw = sinkhorn(
-        dp, protos, teach_rows, teach_cols, part.reshape(dp * stud // 128, 128), raw
+    expo_s, raw, part, kept, teach_rows, high, low = student_pass(packet, stud, teach, head_cols, head_cols.T)
+    targets, totals = sinkhorn(
+        dp, protos, teach_rows, teach_cols, part.reshape(dp * stud // 128, 128)
     )
     totals = totals.reshape(dp, stud)
     aim = dot(head_cols, targets, 1, 1)
-    scaled = (stud_rows.astype(jnp.float32) / totals.reshape(dp * stud, 1)).astype(jnp.bfloat16)
-    high, low = split_sum(sums.T)
+    scaled = (kept.astype(jnp.float32) / totals.reshape(1, dp * stud)).astype(jnp.bfloat16)
     head_grad, raw, aim = weight_pass(
-        dp, protos, scale, expo_s, targets, own_head, scaled.T, high, low, raw, aim
+        dp, protos, scale, expo_s, targets, own_head, scaled, high, low, raw, aim
     )
 
     share = width // protos

time: 410 us -> 345 us (0.84)
  Pallas kernels: 270 us -> 222 us
  local copies, waits for them, and re-layouts: 32.9 us -> 19.4 us
    pallas_call x1, Pallas kernels: 102 us -> 49.7 us  [sinkhorn(): pl.pallas_call(functools.partial(sinkhorn_kernel, dp, protos), in_specs=[...]
    optimization_barrier x1 -> x0, local copies, waits for them, and re-layouts: 8.58 us -> none  [body(): lax.optimization_barrier(lax.all_gather(packet, 'dp', axis=0, tiled=False))]
    unnamed x13 -> x11, local copies, waits for them, and re-layouts: 14.1 us -> 5.77 us
    all_gather x0 -> x1, local copies, waits for them, and re-layouts: none -> 8.36 us  [body(): packet = lax.all_gather(packet, 'dp', axis=0, tiled=False)]
    pallas_call x1 -> x0, local copies, waits for them, and re-layouts: 4.47 us -> none  [student_pass(): pl.pallas_call(student_kernel, grid=(dp,), in_specs=[pl.BlockSpec((1, stu...]
where the time goes in v1:
time: 345 us; the launch traced here: 344 us
  Pallas kernels  222 us (64%)
  waiting for transfers between devices  57.6 us (17%)
  local copies, waits for them, and re-layouts  19.4 us (6%)
  other arithmetic  15.4 us (4%)
  between operations  14.2 us (4%)
  blocking collectives  8.97 us (3%)
  matrix products  6.86 us (2%)
    pallas_call x1, Pallas kernels, weight_pass(): pl.pallas_call(functools.partial(weight_kernel, dp, protos, steps, scale)...  137 us
    all_gather x1, waiting for transfers between devices, body(): packet = lax.all_gather(packet, 'dp', axis=0, tiled=False)  57.6 us
    pallas_call x1, Pallas kernels, sinkhorn(): pl.pallas_call(functools.partial(sinkhorn_kernel, dp, protos), in_specs=[...  49.7 us
    pallas_call x1, Pallas kernels, student_pass(): pl.pallas_call(student_kernel, grid=(dp,), in_specs=[pl.BlockSpec((1, stu...  35 us
    psum x1, blocking collectives, body(): lax.psum(jnp.sum(own_unit * own_part, axis=0, keepdims=True), 'proto')  8.97 us
    all_gather x1, local copies, waits for them, and re-layouts, body(): packet = lax.all_gather(packet, 'dp', axis=0, tiled=False)  8.36 us
  transfers between devices with their start and end apart: 1, of which 1 were waited for; matrix products, arithmetic and copies ran while one was open for 4% of the time, Pallas kernels for 0%

profile of v1, /device:TPU:8, one launch (start us, length us, event | category | flops | bytes accessed | tf_op | source)
XLA Modules:
  0.0 344.2 jit_solution(259258349025761802)
XLA Ops:
  7.2 0.0 copy-start.3
  7.2 0.0 all-gather.3.cloned.1.call-start
  7.2 0.7 fusion.11
  7.9 0.1 broadcast_in_dim.61
  8.0 1.2 copy.24
  9.2 0.1 fusion.4
  9.3 0.1 convert_convert_fusion
  9.4 0.2 copy.26
  9.6 0.2 select_reduce_fusion.1
  9.8 0.1 copy.27
  9.9 0.1 copy.28
  10.0 0.0 copy-done.3
  10.0 0.1 copy.25
  10.1 0.1 fusion.9
  10.2 1.0 pad_maximum_fusion
  11.2 0.0 all-gather.3.cloned.1.call-update
  11.3 3.2 fusion
  14.4 0.0 copy-start
  14.4 2.0 fusion.18
  16.4 4.1 %copy.32.cols_t_ref = bf16[4096,256]{1,0:T(8,128)(2,1)} copy(bf16[4096,256]{0,1:T(8,128)(2,1)} %fusion.18) | data formatting | bytes 4194304 | tf_op jit(solution)/shard_map/transpose | solution.py:499
  20.5 3.5 %fusion.3.cols_ref = bf16[256,4096]{1,0:T(8,128)(2,1)} fusion(f32[4096]{0:T(1024)S(1)} %add_rsqrt_fusion, bf16[256,32768]{1,0:T(8,128)(2,1)} %param.7, s32[]{:T(128)S(6)} %select_n.32), kind=kLoop, calls=%fused_computation.8 | loop fusion | flops 3145728 | bytes 4210692 | tf_op jit(solution)/shard_map/convert_element_type | solution.py:495
  24.0 0.0 copy-done
  24.1 1.8 fusion.1.cols_ref
  25.8 57.6 %all-gather.3.cloned.1.call-done = f32[7168,256]{0,1:T(8,128)} async-done(((f32[896,256]{0,1:T(8,128)}), f32[7168,256]{0,1:T(8,128)}) %all-gather.3.cloned.1.call-update) | async-done | bytes 7340048 | tf_op jit(solution)/shard_map/all_gather | solution.py:494
  83.4 8.4 %copy.37 = f32[7168,256]{1,0:T(8,128)} copy(f32[7168,256]{0,1:T(8,128)} %all-gather.3.cloned.1.call-done) | data formatting | bytes 14680064 | tf_op jit(solution)/shard_map/all_gather | solution.py:494
  91.7 35.0 %student_pass.1 = (bf16[5120,4096]{1,0:T(8,128)(2,1)}, f32[256,5120]{1,0:T(8,128)}, f32[8,5,128]{2,1,0:T(8,128)S(1)}, bf16[256,5120]{1,0:T(8,128)(2,1)}, bf16[10...) custom-call(f32[8,896,256]{2,1,0:T(8,128)} %bitcast.25, ...), custom_call_target="tpu_custom_call" | custom-call | flops 21474836480 | bytes 41943040 | tf_op jit(solution)/shard_map/student_pass/pallas_call | solution.py:101
  126.7 0.0 copy-start.2
  126.7 49.7 %sinkhorn.1 = (bf16[1024,4096]{1,0:T(8,128)(2,1)}, f32[48,128]{1,0:T(8,128)S(1)}) custom-call(bf16[1024,256]{1,0:T(8,128)(2,1)S(1)} %get-tuple-element.15.rows_ref, bf16[256,4096]{1,0:T(8,128)(2,1)} %fusion.3.cols_ref, f32[40,128]{1,0:T(8,128)S(1)} %reshape.57.part_ref), custom_call_target="tpu_custom_call" | custom-call | flops 2147483648 | bytes 16777216 | tf_op jit(solution)/shard_map/sinkhorn/pallas_call | solution.py:273
  176.5 0.0 copy-done.2
  176.5 0.0 copy-start.1
  176.5 6.9 %fusion.15.aim_ref = f32[256,1024]{1,0:T(8,128)} fusion(bf16[256,4096]{1,0:T(8,128)(2,1)S(1)} %copy-done.2, bf16[1024,4096]{1,0:T(8,128)(2,1)} %get-tuple-element.17.targets_ref), kind=kOutput, calls=%fused_computation.43 | convolution fusion | flops 2147483648 | bytes 11534336 | tf_op jit(solution)/shard_map/dot_general | solution.py:33
  183.4 0.0 copy-done.1
  183.4 2.1 divide_convert_fusion.rows_ref
  185.5 137.0 %weight_pass.1 = (f32[32,32768]{1,0:T(8,128)}, f32[64,640]{1,0:T(8,128)S(1)}, f32[64,128]{1,0:T(8,128)S(1)}) custom-call(bf16[5120,4096]{1,0:T(8,128)(2,1)} %get-tuple-element.14.expo_ref, bf16[1024,4096]{1,0:T(8,128)(2,1)} %get-tuple-element.17.targets_ref, bf16[256,4096]{1,0:T(8,128)(2,1)} %copy-done, bf16[256,5120]{1,0:T(8,128)(2,1)} %divide_convert_fusion.rows_ref, ...), custom_call_target="tpu_custom_call" | custom-call | flops 10737418240 | bytes 41943040 | tf_op jit(solution)/shard_map/weight_pass/pallas_call | solution.py:442
  322.4 0.1 reshape.59
  322.5 0.1 fusion.13
  322.6 0.1 copy.33
  322.7 0.1 copy.35
  322.9 0.1 copy.34
  323.0 0.1 copy.36
  323.2 0.1 fusion.5
  323.2 9.0 %psum.7 = f32[640]{0:T(1024)S(1)} all-reduce(f32[640]{0:T(1024)S(1)} %get-tuple-element.28), channel_id=1, replica_groups=mesh['dp'=8,'proto'=4] {'proto'}, use_global_device_ids=true, to_apply=%region_7.8 | all-reduce | flops 640 | bytes 5120 | tf_op jit(solution)/shard_map/psum | solution.py:517
  332.2 0.7 fusion.8
  332.9 4.5 %copy.39 = f32[32,32768]{1,0:T(8,128)} copy(f32[32,32768]{1,0:T(8,128)} %get-tuple-element.42) | data formatting | bytes 8388608
  (11 shorter events, 0.2 us)
Async XLA Ops:
  7.2 2.8 copy-start.3
  7.2 76.2 %all-gather.3.cloned.1.call-start = ((), (), s32[]{:S(2)}) async-start(), calls=%async_computation | async-start | bytes 8257536 | tf_op jit(solution)/shard_map/all_gather | solution.py:494
  14.4 9.6 %copy-start = (bf16[256,4096]{1,0:T(8,128)(2,1)}, bf16[256,4096]{1,0:T(8,128)(2,1)S(1)}, u32[]{:S(2)}) copy-start(bf16[256,4096]{1,0:T(8,128)(2,1)S(1)} %get-tuple-element.31.head_ref) | copy-start | bytes 6291460
  126.7 49.8 %copy-start.2 = (bf16[256,4096]{1,0:T(8,128)(2,1)S(1)}, bf16[256,4096]{1,0:T(8,128)(2,1)}, u32[]{:S(2)}) copy-start(bf16[256,4096]{1,0:T(8,128)(2,1)} %fusion.1.cols_ref) | copy-start | bytes 6291460
  176.5 6.9 %copy-start.1 = (bf16[256,5120]{1,0:T(8,128)(2,1)S(1)}, bf16[256,5120]{1,0:T(8,128)(2,1)}, u32[]{:S(2)}) copy-start(bf16[256,5120]{1,0:T(8,128)(2,1)} %get-tuple-element.18) | copy-start | bytes 7864324
Sparse Core Ops, SparseCore 0:
  11.4 71.9 all-gather.2

commit v2 on v1

--- a/solution.py
+++ b/solution.py
@@ -5,6 +5,7 @@
 import jax.numpy as jnp
 from jax import lax
 from jax.experimental import pallas as pl
+from jax.experimental.layout import Layout, with_layout_constraint
 from jax.experimental.pallas import tpu as pltpu
 from jax.sharding import PartitionSpec as P
 
@@ -58,80 +59,6 @@
 def chunks(size):
     step = min(size, 1024)
     return [(c, step) for c in range(0, size, step)]
-
-
-def student_kernel(
-    rows_ref,
-    teach_ref,
-    sums_ref,
-    cols_ref,
-    cols_t_ref,
-    expo_ref,
-    raw_ref,
-    total_ref,
-    kept_ref,
-    teach_rows_ref,
-    high_ref,
-    low_ref,
-):
-    rows = rows_ref[0].astype(jnp.bfloat16)
-    kept_ref[...] = rows_ref[0].T.astype(jnp.bfloat16)
-    teach_rows_ref[...] = teach_ref[0].astype(jnp.bfloat16)
-    high_ref[...], low_ref[...] = split_sum(sums_ref[0].T)
-    raw, total = None, None
-    for start, step in chunks(cols_ref.shape[1]):
-        logits = dot(rows, cols_ref[:, start : start + step], 1, 0)
-        expo = jnp.exp2(logits * (LOG2E / student_temp))
-        part = jnp.sum(expo, axis=1, keepdims=True)
-        kept = expo.astype(jnp.bfloat16)
-        expo_ref[:, start : start + step] = kept
-        grad = dot(kept, cols_t_ref[start : start + step, :], 1, 0)
-        total = part if total is None else total + part
-        raw = grad if raw is None else raw + grad
-    raw_ref[...] = raw.T
-    for j in range(rows.shape[0] // 128):
-        total_ref[0, j : j + 1, :] = to_lanes(total[j * 128 : (j + 1) * 128])
-
-
-def student_pass(packet, stud, teach, cols, cols_t):
-    dp, _, width = packet.shape
-    first = stud // teach
-    assert stud == first * teach
-    mine = cols.shape[1]
-    return pl.pallas_call(
-        student_kernel,
-        grid=(dp,),
-        in_specs=[
-            pl.BlockSpec((1, stud, width), lambda i: (i, 0, 0)),
-            pl.BlockSpec((1, teach, width), lambda i: (i, first, 0)),
-            pl.BlockSpec((1, teach, width), lambda i: (i, first + 1, 0)),
-            pl.BlockSpec((width, mine), lambda i: (0, 0)),
-            pl.BlockSpec((mine, width), lambda i: (0, 0)),
-        ],
-        out_specs=[
-            pl.BlockSpec((stud, mine), lambda i: (i, 0)),
-            pl.BlockSpec((width, stud), lambda i: (0, i)),
-            pl.BlockSpec((1, stud // 128, 128), lambda i: (i, 0, 0)),
-            pl.BlockSpec((width, stud), lambda i: (0, i)),
-            pl.BlockSpec((teach, width), lambda i: (i, 0)),
-            pl.BlockSpec((width, teach), lambda i: (0, i)),
-            pl.BlockSpec((width, teach), lambda i: (0, i)),
-        ],
-        out_shape=[
-            jax.ShapeDtypeStruct((dp * stud, mine), jnp.bfloat16),
-            jax.ShapeDtypeStruct((width, dp * stud), jnp.float32),
-            jax.ShapeDtypeStruct((dp, stud // 128, 128), jnp.float32),
-            jax.ShapeDtypeStruct((width, dp * stud), jnp.bfloat16),
-            jax.ShapeDtypeStruct((dp * teach, width), jnp.bfloat16),
-            jax.ShapeDtypeStruct((width, dp * teach), jnp.bfloat16),
-            jax.ShapeDtypeStruct((width, dp * teach), jnp.bfloat16),
-        ],
-        compiler_params=pltpu.CompilerParams(vmem_limit_bytes=52 * MIB),
-        cost_estimate=pl.CostEstimate(
-            flops=4 * dp * stud * mine * width, bytes_accessed=2 * dp * stud * mine, transcendentals=dp * stud * mine
-        ),
-        name="student_pass",
-    )(packet, packet, packet, cols, cols_t)
 
 
 def positions():
@@ -179,12 +106,111 @@
         copy.wait()
 
 
+def exchange(here, sizes, axis, buffer, sems):
+    wait_all(start_all(sends(here, sizes, axis, lambda peer: buffer.at[0], lambda k: buffer.at[k], sems)))
+    total = buffer[0]
+    for k in range(1, sizes[axis]):
+        total = total + buffer[k]
+    return total
+
+
+def student_kernel(
+    dp,
+    protos,
+    rows_ref,
+    sums_ref,
+    cols_ref,
+    cols_t_ref,
+    expo_ref,
+    raw_ref,
+    total_ref,
+    kept_ref,
+    high_ref,
+    low_ref,
+    near,
+    far,
+    near_sems,
+    far_sems,
+):
+    turn = pl.program_id(0)
+    rows = rows_ref[0].astype(jnp.bfloat16)
+    kept_ref[...] = rows_ref[0].T.astype(jnp.bfloat16)
+    high_ref[...], low_ref[...] = split_sum(sums_ref[0].T)
+    raw, total = None, None
+    for start, step in chunks(cols_ref.shape[1]):
+        logits = dot(rows, cols_ref[:, start : start + step], 1, 0)
+        expo = jnp.exp2(logits * (LOG2E / student_temp))
+        part = jnp.sum(expo, axis=1, keepdims=True)
+        kept = expo.astype(jnp.bfloat16)
+        expo_ref[:, start : start + step] = kept
+        grad = dot(kept, cols_t_ref[start : start + step, :], 1, 0)
+        total = part if total is None else total + part
+        raw = grad if raw is None else raw + grad
+    raw_ref[...] = raw.T
+    tiles = rows.shape[0] // 128
+    for j in range(tiles):
+        near[0, pl.ds(turn * tiles + j, 1), :] = to_lanes(total[j * 128 : (j + 1) * 128])
+
+    @pl.when(turn == dp - 1)
+    def _():
+        here, sizes = positions(), {"dp": dp, "proto": protos}
+        greet(here, sizes)
+        far[0] = exchange(here, sizes, "proto", near, near_sems)
+        total_ref[...] = exchange(here, sizes, "dp", far, far_sems)
+
+
+def student_pass(protos, packet, stud, teach, cols, cols_t):
+    dp, _, width = packet.shape
+    first = stud // teach
+    count = dp * stud
+    assert stud == first * teach
+    mine = cols.shape[1]
+    return pl.pallas_call(
+        functools.partial(student_kernel, dp, protos),
+        grid=(dp,),
+        in_specs=[
+            pl.BlockSpec((1, stud, width), lambda i: (i, 0, 0)),
+            pl.BlockSpec((1, teach, width), lambda i: (i, first, 0)),
+            pl.BlockSpec((width, mine), lambda i: (0, 0)),
+            pl.BlockSpec((mine, width), lambda i: (0, 0)),
+        ],
+        out_specs=[
+            pl.BlockSpec((stud, mine), lambda i: (i, 0)),
+            pl.BlockSpec((width, stud), lambda i: (0, i)),
+            pl.BlockSpec((count // 128, 128), lambda i: (0, 0)),
+            pl.BlockSpec((width, stud), lambda i: (0, i)),
+            pl.BlockSpec((width, teach), lambda i: (0, i)),
+            pl.BlockSpec((width, teach), lambda i: (0, i)),
+        ],
+        out_shape=[
+            jax.ShapeDtypeStruct((dp * stud, mine), jnp.bfloat16),
+            jax.ShapeDtypeStruct((width, dp * stud), jnp.float32),
+            jax.ShapeDtypeStruct((count // 128, 128), jnp.float32),
+            jax.ShapeDtypeStruct((width, dp * stud), jnp.bfloat16),
+            jax.ShapeDtypeStruct((width, dp * teach), jnp.bfloat16),
+            jax.ShapeDtypeStruct((width, dp * teach), jnp.bfloat16),
+        ],
+        scratch_shapes=[
+            pltpu.VMEM((protos, count // 128, 128), jnp.float32),
+            pltpu.VMEM((dp, count // 128, 128), jnp.float32),
+            pltpu.SemaphoreType.DMA((2, protos)),
+            pltpu.SemaphoreType.DMA((2, dp)),
+        ],
+        compiler_params=pltpu.CompilerParams(
+            collective_id=3, has_side_effects=True, vmem_limit_bytes=52 * MIB
+        ),
+        cost_estimate=pl.CostEstimate(
+            flops=4 * dp * stud * mine * width, bytes_accessed=2 * dp * stud * mine, transcendentals=dp * stud * mine
+        ),
+        name="student_pass",
+    )(packet, packet, cols, cols_t)
+
+
 def sinkhorn_kernel(
     dp,
     protos,
     rows_ref,
     cols_ref,
-    part_ref,
     targets_ref,
     total_ref,
     expo,
@@ -209,28 +235,10 @@
         at = rows_at(block)
         for start, step in chunks(mine):
             values = jnp.exp2(
-                dot(rows_ref[at, :], cols_ref[:, start : start + step], 1, 0) * (LOG2E / teacher_temp)
+                dot(rows_ref[at, :].astype(jnp.bfloat16), cols_ref[:, start : start + step], 1, 0) * (LOG2E / teacher_temp)
             )
             expo[at, start : start + step] = values
             cols[:, start : start + step] += jnp.sum(values, axis=0, keepdims=True)
-
-    def exchange(axis, buffer, sems, it, rows):
-        wait_all(
-            start_all(
-                sends(
-                    here,
-                    sizes,
-                    axis,
-                    lambda peer: buffer.at[it, 0, pl.ds(0, rows)],
-                    lambda k: buffer.at[it, k, pl.ds(0, rows)],
-                    sems.at[it],
-                )
-            )
-        )
-        total = buffer[it, 0, 0:rows]
-        for k in range(1, sizes[axis]):
-            total = total + buffer[it, k, 0:rows]
-        return total
 
     for it in range(ITERS):
         if it:
@@ -249,15 +257,8 @@
             sums = jnp.sum(expo[rows_at(block), :] * cols[...], axis=1, keepdims=True)
             near[it, 0, pl.ds(block, 1), :] = to_lanes(sums)
 
-        used = blocks
-        if it == 0:
-            used = near.shape[2]
-            near[0, 0, blocks:used, :] = part_ref[...]
-        far[it, 0, 0:used] = exchange("proto", near, near_sems, it, used)
-        total = exchange("dp", far, far_sems, it, used)
-        total_ref[0:blocks, :] = 1.0 / total[0:blocks]
-        if it == 0:
-            total_ref[blocks:used, :] = total[blocks:used]
+        far[it, 0] = exchange(here, sizes, "proto", near.at[it], near_sems.at[it])
+        total_ref[...] = 1.0 / exchange(here, sizes, "dp", far.at[it], far_sems.at[it])
 
     @pl.loop(0, blocks)
     def _(block):
@@ -266,13 +267,13 @@
         targets_ref[at, :] = (expo[at, :] * scale * cols[...]).astype(jnp.bfloat16)
 
 
-def sinkhorn(dp, protos, rows, cols, part):
+def sinkhorn(dp, protos, rows, cols):
     count, mine = rows.shape[0], cols.shape[1]
-    used = count // 128 + part.shape[0]
+    used = count // 128
     vmem = pl.BlockSpec(memory_space=pltpu.VMEM)
-    targets, total = pl.pallas_call(
+    return pl.pallas_call(
         functools.partial(sinkhorn_kernel, dp, protos),
-        in_specs=[vmem] * 3,
+        in_specs=[vmem] * 2,
         out_specs=[vmem] * 2,
         out_shape=[
             jax.ShapeDtypeStruct((count, mine), jnp.bfloat16),
@@ -290,11 +291,10 @@
             collective_id=1, has_side_effects=True, vmem_limit_bytes=52 * MIB
         ),
         cost_estimate=pl.CostEstimate(
-            flops=2 * count * mine * rows.shape[1], bytes_accessed=4 * count * mine, transcendentals=count * mine
+            flops=2 * count * mine * rows.shape[1], bytes_accessed=40 * count * mine, transcendentals=count * mine
         ),
         name="sinkhorn",
-    )(rows, cols, part)
-    return targets, total[count // 128 :]
+    )(rows, cols)[0]
 
 
 def weight_kernel(
@@ -490,16 +490,17 @@
     pair_sums = jnp.concatenate(
         [jnp.sum(jnp.where(second, 0.0, kept), 0), jnp.sum(jnp.where(second, kept, 0.0), 0)], 0
     )
-    packet = jnp.concatenate([stud_unit, teach_unit, pair_sums], 0)
+    teach_rows = lax.all_gather(teach_unit, "dp", axis=0, tiled=True)
+    packet = jnp.concatenate([stud_unit, pair_sums], 0)
+    packet, teach_rows = lax.optimization_barrier((packet, teach_rows))
+    packet = with_layout_constraint(packet, Layout(major_to_minor=(0, 1)))
     packet = lax.all_gather(packet, "dp", axis=0, tiled=False)
     teach_cols = unit_columns(lax.dynamic_slice_in_dim(teacher_weight, me * mine, mine, 1))[0].astype(jnp.bfloat16)
     own_head = lax.dynamic_slice_in_dim(head_weight, me * mine, mine, 1)
     head_cols = unit_columns(own_head)[0].astype(jnp.bfloat16)
 
-    expo_s, raw, part, kept, teach_rows, high, low = student_pass(packet, stud, teach, head_cols, head_cols.T)
-    targets, totals = sinkhorn(
-        dp, protos, teach_rows, teach_cols, part.reshape(dp * stud // 128, 128)
-    )
+    targets = sinkhorn(dp, protos, teach_rows, teach_cols)
+    expo_s, raw, totals, kept, high, low = student_pass(protos, packet, stud, teach, head_cols, head_cols.T)
     totals = totals.reshape(dp, stud)
     aim = dot(head_cols, targets, 1, 1)
     scaled = (kept.astype(jnp.float32) / totals.reshape(1, dp * stud)).astype(jnp.bfloat16)

time: 345 us -> 313 us (0.907)
  waiting for transfers between devices: 57.6 us -> 21 us
  Pallas kernels: 222 us -> 231 us
  local copies, waits for them, and re-layouts: 19.4 us -> 12.1 us
    all_gather x1, waiting for transfers between devices: 57.6 us -> 0.01 us  [body(): packet = lax.all_gather(packet, 'dp', axis=0, tiled=False)]
    all_gather x0 -> x1, waiting for transfers between devices: none -> 21 us  [body(): teach_rows = lax.all_gather(teach_unit, 'dp', axis=0, tiled=True)]
    pallas_call x1, Pallas kernels: 35 us -> 45.3 us  [student_pass(): pl.pallas_call(functools.partial(student_kernel, dp, protos), grid=(dp,),...]
    all_gather x1 -> x0, local copies, waits for them, and re-layouts: 8.36 us -> none  [body(): packet = lax.all_gather(packet, 'dp', axis=0, tiled=False)]
  transfers between devices with their start and end apart: 1 -> 2, of which waited for: 1 -> 1; matrix products, arithmetic and copies ran while one was open for 4% -> 8% of each run, Pallas kernels for 0% -> 16%
where the time goes in v2:
time: 313 us
  Pallas kernels  231 us (74%)
  waiting for transfers between devices  21 us (7%)
  other arithmetic  18.8 us (6%)
  between operations  14.3 us (5%)
  local copies, waits for them, and re-layouts  12.1 us (4%)
  blocking collectives  9.03 us (3%)
  matrix products  6.73 us (2%)
    pallas_call x1, Pallas kernels, weight_pass(): pl.pallas_call(functools.partial(weight_kernel, dp, protos, steps, scale)...  136 us
    pallas_call x1, Pallas kernels, sinkhorn(): pl.pallas_call(functools.partial(sinkhorn_kernel, dp, protos), in_specs=[...  48.8 us
    pallas_call x1, Pallas kernels, student_pass(): pl.pallas_call(functools.partial(student_kernel, dp, protos), grid=(dp,),...  45.3 us
    all_gather x1, waiting for transfers between devices, body(): teach_rows = lax.all_gather(teach_unit, 'dp', axis=0, tiled=True)  21 us
    psum x1, blocking collectives, body(): lax.psum(jnp.sum(own_unit * own_part, axis=0, keepdims=True), 'proto')  9.03 us
    dot_general x1, matrix products, dot(): lax.dot_general(a, b, (((da,), (db,)), ((), ())), preferred_element_type=...  6.73 us
  transfers between devices with their start and end apart: 2, of which 1 were waited for; matrix products, arithmetic and copies ran while one was open for 8% of the time, Pallas kernels for 16%

profile of v2, /device:TPU:8, one launch (start us, length us, event | category | flops | bytes accessed | tf_op | source)
XLA Modules:
  0.0 312.5 jit_solution(18030844451902356371)
XLA Ops:
  7.2 0.0 all-gather.4.cloned.1.call-start
  7.2 0.9 fusion.9
  8.2 1.6 convert_multiply_fusion.6
  9.8 0.0 all-gather.4.cloned.1.call-update
  9.8 0.0 all-gather.6.cloned.1.call-start
  9.8 0.7 fusion.11
  10.5 0.1 broadcast_in_dim.61
  10.6 1.2 copy.18
  11.8 0.1 fusion.4
  11.9 0.1 convert_convert_fusion
  12.0 0.2 copy.19
  12.2 0.2 select_reduce_fusion.1
  12.4 0.1 copy.20
  12.5 0.1 copy.21
  12.6 0.1 pad_maximum_fusion
  12.7 21.0 %all-gather.4.cloned.1.call-done.rows_ref = f32[1024,256]{1,0:T(8,128)} async-done(((f32[128,256]{1,0:T(8,128)}), f32[1024,256]{1,0:T(8,128)}) %all-gather.4.cloned.1.call-update) | async-done | bytes 1048592 | tf_op jit(solution)/shard_map/all_gather | solution.py:493
  33.7 1.2 copy.22
  34.9 0.0 all-gather.6.cloned.1.call-update
  34.9 2.1 fusion
  37.0 0.0 copy-start.1
  37.0 2.0 fusion.17
  39.0 4.1 %copy.23.cols_t_ref = bf16[4096,256]{1,0:T(8,128)(2,1)} copy(bf16[4096,256]{0,1:T(8,128)(2,1)} %fusion.17) | data formatting | bytes 4194304 | tf_op jit(solution)/shard_map/transpose | solution.py:503
  43.1 2.4 fusion.2
  45.6 0.0 copy-start
  45.6 3.5 %fusion.3.cols_ref = bf16[256,4096]{1,0:T(8,128)(2,1)} fusion(f32[4096]{0:T(1024)S(1)} %add_rsqrt_fusion, bf16[256,32768]{1,0:T(8,128)(2,1)} %param.7, s32[]{:T(128)S(6)} %select_n.32), kind=kLoop, calls=%fused_computation.8 | loop fusion | flops 3145728 | bytes 4210692 | tf_op jit(solution)/shard_map/convert_element_type | solution.py:498
  49.0 0.0 copy-done.1
  49.0 0.5 fusion.1.cols_ref
  49.5 0.0 copy-done
  49.5 0.0 copy-start.2
  49.5 48.8 %sinkhorn.1 = (bf16[1024,4096]{1,0:T(8,128)(2,1)}, f32[8,128]{1,0:T(8,128)}) custom-call(f32[1024,256]{1,0:T(8,128)S(1)} %copy-done, bf16[256,4096]{1,0:T(8,128)(2,1)} %fusion.3.cols_ref), custom_call_target="tpu_custom_call" | custom-call | flops 2147483648 | bytes 167772160 | tf_op jit(solution)/shard_map/sinkhorn/pallas_call | solution.py:274
  98.3 0.0 copy-done.2
  98.4 6.7 %fusion.14.aim_ref = f32[256,1024]{1,0:T(8,128)} fusion(bf16[256,4096]{1,0:T(8,128)(2,1)S(1)} %fusion.1.cols_ref, bf16[1024,4096]{1,0:T(8,128)(2,1)} %get-tuple-element.17.targets_ref), kind=kOutput, calls=%fused_computation.41 | convolution fusion | flops 2147483648 | bytes 11534336 | tf_op jit(solution)/shard_map/dot_general | solution.py:34
  105.1 0.0 all-gather.6.cloned.1.call-done
  105.1 45.3 %student_pass.1 = (bf16[5120,4096]{1,0:T(8,128)(2,1)}, f32[256,5120]{1,0:T(8,128)}, f32[40,128]{1,0:T(8,128)S(1)}, bf16[256,5120]{1,0:T(8,128)(2,1)}, bf16[256,1...) custom-call(f32[8,768,256]{2,1,0:T(8,128)} %bitcast.30, f32[8,768,256]{2,1,0:T(8,128)} %bitcast.31, ...), custom_call_target="tpu_custom_call" | custom-call | flops 21474836480 | bytes 41943040 | tf_op jit(solution)/shard_map/student_pass/pallas_call | solution.py:168
  150.4 3.8 %divide_convert_fusion.rows_ref = bf16[256,5120]{1,0:T(8,128)(2,1)} fusion(bf16[256,5120]{1,0:T(8,128)(2,1)} %get-tuple-element.18, f32[5120]{0:T(1024)S(1)} %bitcast.24), kind=kLoop, calls=%fused_computation.4 | loop fusion | flops 3932160 | bytes 5263360 | tf_op jit(solution)/shard_map/convert_element_type | solution.py:506
  154.2 136.5 %weight_pass.1 = (f32[32,32768]{1,0:T(8,128)}, f32[64,640]{1,0:T(8,128)S(1)}, f32[64,128]{1,0:T(8,128)S(1)}) custom-call(bf16[5120,4096]{1,0:T(8,128)(2,1)} %get-tuple-element.15.expo_ref, bf16[1024,4096]{1,0:T(8,128)(2,1)} %get-tuple-element.17.targets_ref, bf16[256,4096]{1,0:T(8,128)(2,1)} %copy-done.1, bf16[256,5120]{1,0:T(8,128)(2,1)} %divide_convert_fusion.rows_ref, ...), custom_call_target="tpu_custom_call" | custom-call | flops 10737418240 | bytes 41943040 | tf_op jit(solution)/shard_map/weight_pass/pallas_call | solution.py:442
  290.7 0.1 reshape.55
  290.8 0.1 fusion.13
  290.9 0.1 copy.24
  291.0 0.1 copy.26
  291.1 0.1 copy.25
  291.2 0.1 copy.27
  291.4 0.1 fusion.5
  291.5 9.0 %psum.7 = f32[640]{0:T(1024)S(1)} all-reduce(f32[640]{0:T(1024)S(1)} %get-tuple-element.28), channel_id=1, replica_groups=mesh['dp'=8,'proto'=4] {'proto'}, use_global_device_ids=true, to_apply=%region_7.8 | all-reduce | flops 640 | bytes 5120 | tf_op jit(solution)/shard_map/psum | solution.py:518
  300.5 0.7 fusion.8
  301.2 4.5 %copy.29 = f32[32,32768]{1,0:T(8,128)} copy(f32[32,32768]{1,0:T(8,128)} %get-tuple-element.39) | data formatting | bytes 8388608
  (8 shorter events, 0.1 us)
Async XLA Ops:
  7.2 26.5 %all-gather.4.cloned.1.call-start = ((), (), s32[]{:S(2)}) async-start(), calls=%async_computation | async-start | bytes 1179648 | tf_op jit(solution)/shard_map/all_gather | solution.py:493
  9.8 95.3 %all-gather.6.cloned.1.call-start = ((), (), s32[]{:S(2)}) async-start(), calls=%async_computation.1 | async-start | bytes 7077888 | tf_op jit(solution)/shard_map/all_gather | solution.py:497
  37.0 12.0 %copy-start.1 = (bf16[256,4096]{1,0:T(8,128)(2,1)}, bf16[256,4096]{1,0:T(8,128)(2,1)S(1)}, u32[]{:S(2)}) copy-start(bf16[256,4096]{1,0:T(8,128)(2,1)S(1)} %get-tuple-element.31.head_ref) | copy-start | bytes 6291460
  45.6 3.9 %copy-start = (f32[1024,256]{1,0:T(8,128)S(1)}, f32[1024,256]{1,0:T(8,128)}, u32[]{:S(2)}) copy-start(f32[1024,256]{1,0:T(8,128)} %all-gather.4.cloned.1.call-done.rows_ref) | copy-start | bytes 3145732
  49.5 48.8 %copy-start.2 = (bf16[256,4096]{1,0:T(8,128)(2,1)}, bf16[256,4096]{1,0:T(8,128)(2,1)S(1)}, u32[]{:S(2)}) copy-start(bf16[256,4096]{1,0:T(8,128)(2,1)S(1)} %fusion.1.cols_ref) | copy-start | bytes 6291460
Sparse Core Ops, SparseCore 0:
  10.2 23.4 all-gather.3
  35.3 63.4 all-gather.5

commit v3 on v2

--- a/solution.py
+++ b/solution.py
@@ -492,15 +492,18 @@
     )
     teach_rows = lax.all_gather(teach_unit, "dp", axis=0, tiled=True)
     packet = jnp.concatenate([stud_unit, pair_sums], 0)
-    packet, teach_rows = lax.optimization_barrier((packet, teach_rows))
-    packet = with_layout_constraint(packet, Layout(major_to_minor=(0, 1)))
-    packet = lax.all_gather(packet, "dp", axis=0, tiled=False)
     teach_cols = unit_columns(lax.dynamic_slice_in_dim(teacher_weight, me * mine, mine, 1))[0].astype(jnp.bfloat16)
     own_head = lax.dynamic_slice_in_dim(head_weight, me * mine, mine, 1)
     head_cols = unit_columns(own_head)[0].astype(jnp.bfloat16)
+    head_cols_t = head_cols.T
+    packet, teach_rows, teach_cols, head_cols, head_cols_t, own_head = lax.optimization_barrier(
+        (packet, teach_rows, teach_cols, head_cols, head_cols_t, own_head)
+    )
+    packet = with_layout_constraint(packet, Layout(major_to_minor=(0, 1)))
+    packet = lax.all_gather(packet, "dp", axis=0, tiled=False)
 
     targets = sinkhorn(dp, protos, teach_rows, teach_cols)
-    expo_s, raw, totals, kept, high, low = student_pass(protos, packet, stud, teach, head_cols, head_cols.T)
+    expo_s, raw, totals, kept, high, low = student_pass(protos, packet, stud, teach, head_cols, head_cols_t)
     totals = totals.reshape(dp, stud)
     aim = dot(head_cols, targets, 1, 1)
     scaled = (kept.astype(jnp.float32) / totals.reshape(1, dp * stud)).astype(jnp.bfloat16)

time: 313 us -> 309 us (0.987)
  waiting for transfers between devices: 21 us -> 10.3 us
    all_gather x1, waiting for transfers between devices: 21 us -> 6.35 us  [body(): teach_rows = lax.all_gather(teach_unit, 'dp', axis=0, tiled=True)]
    optimization_barrier x1 -> x2, local copies, waits for them, and re-layouts: 1.17 us -> 5.43 us  [body(): lax.optimization_barrier((packet, teach_rows, teach_cols, head_cols, head...]
    transpose x1 -> x0, local copies, waits for them, and re-layouts: 4.1 us -> none  [body(): expo_s, raw, totals, kept, high, low = student_pass(protos, packet, stud,...]
    all_gather x1, waiting for transfers between devices: 0.01 us -> 3.89 us  [body(): packet = lax.all_gather(packet, 'dp', axis=0, tiled=False)]
    convert_element_type x1 -> x0, other arithmetic: 3.46 us -> none  [body(): unit_columns(lax.dynamic_slice_in_dim(teacher_weight, me * mine, mine, 1))]
    pallas_call x1, Pallas kernels: 45.3 us -> 48.4 us  [student_pass(): pl.pallas_call(functools.partial(student_kernel, dp, protos), grid=(dp,),...]
  transfers between devices with their start and end apart: 2 -> 2, of which waited for: 1 -> 2; matrix products, arithmetic and copies ran while one was open for 8% -> 9% of each run, Pallas kernels for 16% -> 16%
where the time goes in v3:
time: 309 us
  Pallas kernels  233 us (75%)
  other arithmetic  20.3 us (7%)
  local copies, waits for them, and re-layouts  14.5 us (5%)
  between operations  14.3 us (5%)
  waiting for transfers between devices  10.3 us (3%)
  blocking collectives  9.32 us (3%)
  matrix products  7.05 us (2%)
    pallas_call x1, Pallas kernels, weight_pass(): pl.pallas_call(functools.partial(weight_kernel, dp, protos, steps, scale)...  136 us
    pallas_call x1, Pallas kernels, sinkhorn(): pl.pallas_call(functools.partial(sinkhorn_kernel, dp, protos), in_specs=[...  48.7 us
    pallas_call x1, Pallas kernels, student_pass(): pl.pallas_call(functools.partial(student_kernel, dp, protos), grid=(dp,),...  48.4 us
    psum x1, blocking collectives, body(): lax.psum(jnp.sum(own_unit * own_part, axis=0, keepdims=True), 'proto')  9.32 us
    dot_general x1, matrix products, dot(): lax.dot_general(a, b, (((da,), (db,)), ((), ())), preferred_element_type=...  7.05 us
    reduce_sum x2, other arithmetic, unit_columns(): jnp.sum(floats * floats, axis=0, keepdims=True) + tiny_eps  6.68 us
    all_gather x1, waiting for transfers between devices, body(): teach_rows = lax.all_gather(teach_unit, 'dp', axis=0, tiled=True)  6.35 us
  transfers between devices with their start and end apart: 2, of which 2 were waited for; matrix products, arithmetic and copies ran while one was open for 9% of the time, Pallas kernels for 16%

profile of v3, /device:TPU:8, one launch (start us, length us, event | category | flops | bytes accessed | tf_op | source)
XLA Modules:
  0.0 308.9 jit_solution(3928385108257858145)
XLA Ops:
  7.2 0.0 all-gather.4.cloned.1.call-start
  7.2 0.9 fusion.9
  8.2 1.6 convert_multiply_fusion.6
  9.8 0.0 all-gather.4.cloned.1.call-update
  9.8 0.0 all-gather.6.cloned.1.call-start
  9.8 2.0 fusion
  11.9 0.0 copy-start.8
  11.9 0.0 copy-start.3
  11.9 4.6 %fusion.2 = (f32[4096]{0:T(1024)S(1)}, bf16[256,4096]{1,0:T(8,128)(2,1)S(1)}, bf16[256,4096]{1,0:T(8,128)(2,1)}) fusion(bf16[256,32768]{1,0:T(8,128)(2,1)} %param.8, s32[]{:T(128)S(6)} %select_n.32, f32[4096]{0:T(1024)S(1)} %add_rsqrt_fusion.1, bf16[256,32768]{1,0:T(8,128)(2,1)} %param.7), kind=kLoop, calls=%fused_computation.7 | loop fusion | flops 6287360 | bytes 8421380 | tf_op jit(solution)/shard_map/reduce_sum | solution.py:29
  16.6 0.0 copy-start.1
  16.6 0.0 copy-done.8
  16.6 0.0 copy-start.6
  16.6 0.8 broadcast_in_dim.61
  17.4 0.0 copy-done.3
  17.4 0.2 copy.18
  17.6 0.1 fusion.4
  17.7 0.0 copy-done.6
  17.7 0.0 copy-start.4
  17.7 0.9 convert_convert_fusion
  18.7 0.0 copy-done.4
  18.7 1.4 copy.19
  20.1 0.9 select_reduce_fusion.1
  20.9 0.7 copy.20
  21.7 0.8 copy.21
  22.4 1.1 pad_maximum_fusion
  23.5 1.7 fusion.17
  25.3 0.0 copy-done.1
  25.3 1.8 fusion.3.cols_ref
  27.1 6.4 %all-gather.4.cloned.1.call-done.rows_ref = f32[1024,256]{1,0:T(8,128)} async-done(((f32[128,256]{1,0:T(8,128)}), f32[1024,256]{1,0:T(8,128)}) %all-gather.4.cloned.1.call-update) | async-done | bytes 1048592 | tf_op jit(solution)/shard_map/all_gather | solution.py:493
  33.4 0.0 copy-start
  33.4 1.2 copy.22
  34.6 0.0 all-gather.6.cloned.1.call-update
  34.6 4.3 %copy.23.cols_t_ref = bf16[4096,256]{1,0:T(8,128)(2,1)} copy(bf16[4096,256]{0,1:T(8,128)(2,1)} %fusion.17) | data formatting | bytes 4194304 | tf_op jit(solution)/shard_map/optimization_barrier | solution.py:499
  38.9 0.0 copy-done
  38.9 0.0 copy-start.2
  38.9 48.7 %sinkhorn.1 = (bf16[1024,4096]{1,0:T(8,128)(2,1)}, f32[8,128]{1,0:T(8,128)}) custom-call(f32[1024,256]{1,0:T(8,128)S(1)} %copy-done, bf16[256,4096]{1,0:T(8,128)(2,1)} %get-tuple-element.23.cols_ref), custom_call_target="tpu_custom_call" | custom-call | flops 2147483648 | bytes 167772160 | tf_op jit(solution)/shard_map/sinkhorn/pallas_call | solution.py:274
  87.6 0.0 copy-done.2
  87.6 7.1 %fusion.14.aim_ref = f32[256,1024]{1,0:T(8,128)} fusion(bf16[256,4096]{1,0:T(8,128)(2,1)S(1)} %copy-done.2, bf16[1024,4096]{1,0:T(8,128)(2,1)} %get-tuple-element.24.targets_ref), kind=kOutput, calls=%fused_computation.41 | convolution fusion | flops 2147483648 | bytes 11534336 | tf_op jit(solution)/shard_map/dot_general | solution.py:34
  94.6 3.9 %all-gather.6.cloned.1.call-done = f32[6144,256]{1,0:T(8,128)} async-done(((f32[768,256]{1,0:T(8,128)}), f32[6144,256]{1,0:T(8,128)}) %all-gather.6.cloned.1.call-update) | async-done | bytes 6291472 | tf_op jit(solution)/shard_map/all_gather | solution.py:503
  98.5 48.4 %student_pass.1 = (bf16[5120,4096]{1,0:T(8,128)(2,1)}, f32[256,5120]{1,0:T(8,128)}, f32[40,128]{1,0:T(8,128)S(1)}, bf16[256,5120]{1,0:T(8,128)(2,1)}, bf16[256,1...) custom-call(f32[8,768,256]{2,1,0:T(8,128)} %bitcast.30, f32[8,768,256]{2,1,0:T(8,128)} %bitcast.31, ...), custom_call_target="tpu_custom_call" | custom-call | flops 21474836480 | bytes 41943040 | tf_op jit(solution)/shard_map/student_pass/pallas_call | solution.py:168
  146.9 3.8 %divide_convert_fusion.rows_ref = bf16[256,5120]{1,0:T(8,128)(2,1)} fusion(bf16[256,5120]{1,0:T(8,128)(2,1)} %get-tuple-element.26, f32[5120]{0:T(1024)S(1)} %bitcast.24), kind=kLoop, calls=%fused_computation.4 | loop fusion | flops 3932160 | bytes 5263360 | tf_op jit(solution)/shard_map/convert_element_type | solution.py:509
  150.8 0.0 copy-start.7
  150.8 0.0 copy-start.5
  150.8 136.0 %weight_pass.1 = (f32[32,32768]{1,0:T(8,128)}, f32[64,640]{1,0:T(8,128)S(1)}, f32[64,128]{1,0:T(8,128)S(1)}) custom-call(bf16[5120,4096]{1,0:T(8,128)(2,1)} %get-tuple-element.21.expo_ref, bf16[1024,4096]{1,0:T(8,128)(2,1)} %get-tuple-element.24.targets_ref, bf16[256,4096]{1,0:T(8,128)(2,1)} %copy-done.1, bf16[256,5120]{1,0:T(8,128)(2,1)} %divide_convert_fusion.rows_ref, ...), custom_call_target="tpu_custom_call" | custom-call | flops 10737418240 | bytes 41943040 | tf_op jit(solution)/shard_map/weight_pass/pallas_call | solution.py:442
  286.8 0.1 reshape.55
  286.9 0.1 fusion.13
  287.0 0.1 copy.24
  287.1 0.1 copy.26
  287.2 0.1 copy.25
  287.4 0.1 copy.27
  287.5 0.0 copy-done.7
  287.5 0.1 fusion.5
  287.6 9.3 %psum.7 = f32[640]{0:T(1024)S(1)} all-reduce(f32[640]{0:T(1024)S(1)} %get-tuple-element.36), channel_id=1, replica_groups=mesh['dp'=8,'proto'=4] {'proto'}, use_global_device_ids=true, to_apply=%region_7.8 | all-reduce | flops 640 | bytes 5120 | tf_op jit(solution)/shard_map/psum | solution.py:521
  296.9 0.0 copy-done.5
  296.9 0.7 fusion.8
  297.6 4.5 %copy.29 = f32[32,32768]{1,0:T(8,128)} copy(f32[32,32768]{1,0:T(8,128)} %get-tuple-element.48) | data formatting | bytes 8388608
  (9 shorter events, 0.1 us)
Async XLA Ops:
  7.2 26.2 %all-gather.4.cloned.1.call-start = ((), (), s32[]{:S(2)}) async-start(), calls=%async_computation | async-start | bytes 1179648 | tf_op jit(solution)/shard_map/all_gather | solution.py:493
  9.8 88.7 %all-gather.6.cloned.1.call-start = ((), (), s32[]{:S(2)}) async-start(), calls=%async_computation.1 | async-start | bytes 7077888 | tf_op jit(solution)/shard_map/all_gather | solution.py:503
  11.9 4.7 %copy-start.8 = (s32[640]{0:T(1024)S(1)}, s32[640]{0:T(1024)}, u32[]{:S(2)}) copy-start(s32[640]{0:T(1024)} %param.9) | copy-start | bytes 7684
  11.9 5.5 %copy-start.3 = (bf16[640,256]{1,0:T(8,128)(2,1)S(1)}, bf16[640,256]{1,0:T(8,128)(2,1)}, u32[]{:S(2)}) copy-start(bf16[640,256]{1,0:T(8,128)(2,1)} %param.6) | copy-start | bytes 983044
  16.6 8.7 %copy-start.1 = (bf16[256,4096]{1,0:T(8,128)(2,1)}, bf16[256,4096]{1,0:T(8,128)(2,1)S(1)}, u32[]{:S(2)}) copy-start(bf16[256,4096]{1,0:T(8,128)(2,1)S(1)} %get-tuple-element.25.head_ref) | copy-start | bytes 6291460
  16.6 1.1 copy-start.6
  17.7 1.0 copy-start.4
  33.4 5.5 %copy-start = (f32[1024,256]{1,0:T(8,128)S(1)}, f32[1024,256]{1,0:T(8,128)}, u32[]{:S(2)}) copy-start(f32[1024,256]{1,0:T(8,128)} %all-gather.4.cloned.1.call-done.rows_ref) | copy-start | bytes 3145732
  38.9 48.7 %copy-start.2 = (bf16[256,4096]{1,0:T(8,128)(2,1)S(1)}, bf16[256,4096]{1,0:T(8,128)(2,1)}, u32[]{:S(2)}) copy-start(bf16[256,4096]{1,0:T(8,128)(2,1)} %fusion.3.cols_ref) | copy-start | bytes 6291460
  150.8 136.8 %copy-start.7 = (pred[640]{0:T(1024)(128)(4,1)S(1)}, pred[640]{0:T(1024)(128)(4,1)}, u32[]{:S(2)}) copy-start(pred[640]{0:T(1024)(128)(4,1)} %copy-done.6) | copy-start | bytes 1924
  150.8 146.2 %copy-start.5 = (f32[640]{0:T(1024)S(1)}, f32[640]{0:T(1024)}, u32[]{:S(2)}) copy-start(f32[640]{0:T(1024)} %copy-done.4) | copy-start | bytes 7684
Sparse Core Ops, SparseCore 0:
  9.9 23.4 all-gather.3
  35.0 63.4 all-gather.5
